TPU v7x, 32 devices: a whole 2x2x4 slice. The times are simulated.
32 devices in a mesh: py: 4 (over z), pz: 8 (over y, x, core).
Axes of the slice: x: 2, y: 2, z: 4, core: 2. Of those that a mesh axis runs over, the one named last changes fastest.
Arguments:
- vort_p: bfloat16 [3, 131072], P(None, ('py', 'pz')), may hold values from -6 to 6
- pair_weights: bfloat16 [8192, 64, 128], P(('py', 'pz')), may hold values from -1.796875 to 1.796875
- pair_part: int32 [8192], P(('py', 'pz')), may hold values from 0 to 31
- pair_node: int32 [8192], P(('py', 'pz')), may hold values from 0 to 95, as said below
- counts: int32 [32], P(('py', 'pz')), may hold values from 128 to 256, as said below
Outputs:
- vel_p: float32 [3, 131072], P(None, ('py', 'pz'))
Inputs may be any that keep to these rules, and one draw needn't show every extreme that they name: `counts`: every pencil has at least 128 live slots, and some pencil has all 256 slots live in every draw. `pair_node`: in every pencil the slots below 96 name each of its node blocks exactly once.
All inputs are finite; a program needn't handle non-finite values.
Results may differ from a plain program's by a relative error of at most 0.0029.
Values sent between devices are 32-bit elements; how exact they have to be, the bound alone decides.
A program may use at most 64 MiB of HBM per device.

v0:
```python
import functools
import math

import jax
import jax.numpy as jnp
import numpy as np
from jax import lax
from jax.experimental import pallas as pl
from jax.experimental.pallas import tpu as pltpu
from jax.sharding import PartitionSpec as P

NX = 384
CY = 8
CZ = 2
BP = 128
BN = 64
PB_DEV = 32
ROWS = 8
CHUNK = 32
GROUP = 4
MESH = pl.DeviceIdType.MESH
f32 = jnp.float32
bf16 = jnp.bfloat16


def twiddle(row_index, col_index, period):
    product = row_index[:, None] * col_index[None, :] % period
    return product.astype(jnp.float32) * (2.0 * math.pi / period)


def forward_table(length):
    angle = twiddle(jnp.arange(length), jnp.arange(length), length)
    cosine = jnp.cos(angle)
    sines = jnp.sin(angle)
    return jnp.stack([jnp.stack([cosine, -sines], 1), jnp.stack([sines, cosine], 1)], 0)


def inverse_table(length):
    angle = twiddle(jnp.arange(length), jnp.arange(length), length)
    cosine = jnp.cos(angle) / length
    sines = jnp.sin(angle) / length
    return jnp.stack([jnp.stack([cosine, sines], 1), jnp.stack([-sines, cosine], 1)], 0)


def cross_terms(coeffs, field):
    return jnp.stack(
        [
            coeffs[1] * field[2] - coeffs[2] * field[1],
            coeffs[2] * field[0] - coeffs[0] * field[2],
            coeffs[0] * field[1] - coeffs[1] * field[0],
        ],
        axis=0,
    )


def signed_wave(length, index):
    signed = jnp.where(index < length // 2, index, index - length)
    return (signed.astype(jnp.float32) * (2.0 * math.pi / length), index == length // 2)


def curl_solve(spectrum, y_cells, z_cells):
    x_local = spectrum.shape[1]
    y_local = spectrum.shape[3]
    mode_x = lax.axis_index("py") * x_local + jnp.arange(x_local)
    wave_x = mode_x.astype(jnp.float32) * (2.0 * math.pi / NX)
    wave_y, edge_y = signed_wave(y_cells, lax.axis_index("pz") * y_local + jnp.arange(y_local))
    wave_z, edge_z = signed_wave(z_cells, jnp.arange(z_cells))
    wave_x3 = wave_x[:, None, None]
    wave_y3 = wave_y[None, :, None]
    wave_z3 = wave_z[None, None, :]
    total = wave_x3 * wave_x3 + wave_y3 * wave_y3 + wave_z3 * wave_z3
    edges = edge_y[None, :, None] | edge_z[None, None, :]
    keep = (total > 0) & jnp.logical_not(edges)
    inverse_sq = jnp.where(keep, 1.0 / jnp.where(keep, total, 1.0), 0.0)
    inv_wave = (wave_x3 * inverse_sq, wave_y3 * inverse_sq, wave_z3 * inverse_sq)
    real_turn = cross_terms(inv_wave, spectrum[:, :, 0])
    imag_turn = cross_terms(inv_wave, spectrum[:, :, 1])
    return jnp.stack([-imag_turn, real_turn], axis=2)


def halves(table):
    table = np.asarray(table, np.float32)
    high = table.astype(bf16)
    return high, (table - high.astype(np.float32)).astype(bf16)


def split(x):
    high = x.astype(bf16)
    return high, (x - high.astype(f32)).astype(bf16)


def dot(a, b, dims=((1,), (0,))):
    return lax.dot_general(a, b, (dims, ((), ())), preferred_element_type=f32)


def left_half(shape):
    return lax.broadcasted_iota(jnp.int32, shape, 1) < BN


def spread_kernel(part, node, count, parts_ref, w_ref, out_ref, near_ref, parts, sems):
    chunks = w_ref.shape[0] // CHUNK

    def fetch(k):
        here = pl.ds(k * CHUNK, CHUNK)
        return pltpu.make_async_copy(w_ref.at[here], near_ref.at[here], sems.at[k])

    for k in range(chunks):
        fetch(k).start()
    out_ref[...] = jnp.zeros_like(out_ref)
    parts[...] = jnp.zeros_like(parts)
    for b in range(PB_DEV):
        parts[b, 0:3, :] = parts_ref[:, b * BP : (b + 1) * BP].astype(f32)
    left = left_half((ROWS, 128))

    def chunk(k, carry):
        fetch(k).wait()
        base = k * CHUNK
        for g in range(CHUNK // GROUP):
            first = base + g * GROUP
            picked = jnp.concatenate([parts[part[first + i]] for i in range(GROUP)], axis=0)
            tiles = near_ref[pl.ds(first, GROUP)].reshape(GROUP * BN, BP)
            got = dot(picked.astype(bf16), tiles, ((1,), (1,)))
            for i in range(GROUP):
                keep = jnp.logical_and(left if i % 2 == 0 else ~left, first + i < count[0])
                lanes = i // 2 * 128
                own = got[i * ROWS : (i + 1) * ROWS, lanes : lanes + 128]
                out_ref[node[first + i]] += jnp.where(keep, own, 0.0)
        return carry

    lax.fori_loop(0, chunks, chunk, 0)


def spread(vort_p, weights, part, node, counts, node_blocks):
    smem = pl.BlockSpec(memory_space=pltpu.SMEM)
    vmem = pl.BlockSpec(memory_space=pltpu.VMEM)
    return pl.pallas_call(
        spread_kernel,
        out_shape=(
            jax.ShapeDtypeStruct((node_blocks, ROWS, 2 * BN), f32),
            jax.ShapeDtypeStruct(weights.shape, weights.dtype),
        ),
        in_specs=[smem, smem, smem, vmem, pl.BlockSpec(memory_space=pltpu.HBM)],
        out_specs=(vmem, vmem),
        scratch_shapes=[
            pltpu.VMEM((PB_DEV, ROWS, BP), f32),
            pltpu.SemaphoreType.DMA((weights.shape[0] // CHUNK,)),
        ],
        compiler_params=pltpu.CompilerParams(vmem_limit_bytes=48 * 2**20),
        name="spread",
    )(part, node, counts, vort_p, weights)


def collect_kernel(part, node, count, vel_ref, w_ref, out_ref, sums):
    sums[...] = jnp.zeros_like(sums)
    left = left_half((ROWS, 128))
    zero = jnp.zeros((ROWS, 128), f32)

    def chunk(k, carry):
        for g in range(CHUNK // GROUP):
            first = k * CHUNK + g * GROUP
            rows = []
            for i in range(GROUP):
                slot = first + i
                keep = jnp.logical_and(left if i % 2 == 0 else ~left, slot < count[0])
                own = jnp.where(keep, vel_ref[node[slot]], 0.0)
                rows.append(
                    jnp.concatenate(
                        [own if h == i // 2 else zero for h in range(GROUP // 2)], axis=1
                    )
                )
            chosen = jnp.concatenate(rows, axis=0).astype(bf16)
            got = dot(chosen, w_ref[pl.ds(first, GROUP)].reshape(GROUP * BN, BP))
            for i in range(GROUP):
                sums[part[first + i]] += got[i * ROWS : (i + 1) * ROWS]
        return carry

    lax.fori_loop(0, w_ref.shape[0] // CHUNK, chunk, 0)
    for b in range(PB_DEV):
        out_ref[:, b * BP : (b + 1) * BP] = sums[b, 0:3, :]


def collect(vel, weights, part, node, counts):
    smem = pl.BlockSpec(memory_space=pltpu.SMEM)
    vmem = pl.BlockSpec(memory_space=pltpu.VMEM)
    return pl.pallas_call(
        collect_kernel,
        out_shape=jax.ShapeDtypeStruct((3, PB_DEV * BP), f32),
        in_specs=[smem, smem, smem, vmem, vmem],
        out_specs=vmem,
        scratch_shapes=[pltpu.VMEM((PB_DEV, ROWS, BP), f32)],
        compiler_params=pltpu.CompilerParams(vmem_limit_bytes=24 * 2**20),
        name="collect",
    )(part, node, counts, vel, weights)


def tables(n_py, n_pz):
    devices = n_py * n_pz
    local = NX // 2 // devices
    ny, nz = CY * n_py, CZ * n_pz
    row = np.arange(devices * ROWS)
    slot, device = row % ROWS, row // ROWS
    mode = device * local + slot
    angle = 2 * np.pi * (mode[:, None] * np.arange(NX)[None] % NX) / NX
    used = (slot < local)[:, None]
    x_cos, x_sin = np.where(used, np.cos(angle), 0.0), np.where(used, -np.sin(angle), 0.0)
    index = np.arange(devices)
    a, b = index // n_pz, index % n_pz
    theta = 2 * np.pi * (a[:, None] * a[None] / n_py + b[:, None] * b[None] / n_pz)
    eye = np.eye(ROWS)
    far = np.concatenate([np.kron(np.cos(theta), eye), np.kron(np.sin(theta), eye)], 0)
    lane = np.arange(128)
    real, comp, cell = lane // 64, lane % 64 // 16, lane % 16
    zl, yl = cell // CY, cell % CY
    valid = (comp < 3)[None]
    phi = 2 * np.pi * (a[:, None] * yl[None] / ny + b[:, None] * zl[None] / nz)
    sign = np.where(real == 0, 1.0, -1.0)[None]
    turn_cos, turn_sin = np.cos(phi), np.sin(phi) * sign
    psi = 2 * np.pi * (yl[:, None] * yl[None] / CY + zl[:, None] * zl[None] / CZ)

    def near(ahead):
        cosine, sines = np.cos(psi), np.sin(psi)
        r, q = real[:, None], real[None]
        both = np.where(r == q, sines, np.where(r == 0, cosine, -cosine))
        same = (comp[:, None] == (comp[None] + ahead) % 3) & (comp[:, None] < 3) & valid
        return np.where(same, both, 0.0)

    forward = np.concatenate([near(2), near(1)], 1)
    cosine, sines = np.cos(psi), np.sin(psi)
    r, q = real[:, None], real[None]
    both = np.where(r == q, cosine, np.where(r == 0, sines, -sines))
    same = (comp[:, None] == comp[None]) & (comp[:, None] < 3)
    back = np.where(same, both, 0.0)
    my, mz = a[:, None] + n_py * yl[None], b[:, None] + n_pz * zl[None]
    keep = (my != ny // 2) & (mz != nz // 2) & valid
    my, mz = np.where(my < ny // 2, my, my - ny), np.where(mz < nz // 2, mz, mz - nz)
    ky, kz = 2 * np.pi * my / ny, 2 * np.pi * mz / nz
    zero = np.zeros_like(ky)
    wave = np.stack([zero, ky, kz])
    k_first = np.where(comp == 0, wave[1], np.where(comp == 1, wave[2], wave[0]))
    k_second = np.where(comp == 0, wave[2], np.where(comp == 1, wave[0], wave[1]))
    x_first = np.broadcast_to(comp == 2, ky.shape)
    x_second = np.broadcast_to(comp == 1, ky.shape)
    small = [turn_cos, turn_sin, ky * ky + kz * kz, k_first, k_second, x_first, x_second, keep]
    small = np.stack(small).astype(np.float32)
    return [
        *halves(np.stack([x_cos, x_sin])),
        *halves(far),
        *halves(forward),
        *halves(back),
        small,
    ]


def solve_kernel(
    n_py,
    n_pz,
    count,
    part_ref,
    node_ref,
    parts_ref,
    w_ref,
    *rest_refs,
):
    n_consts = 9
    consts, out_ref = rest_refs[:n_consts], rest_refs[n_consts]
    held = rest_refs[n_consts + 1 : 2 * n_consts + 1]
    (
        near_ref,
        vel_ref,
        send_a,
        recv_a,
        send_b,
        recv_b,
        send_sem,
        recv_sem,
        parts,
        picks,
        pairs,
        sems,
        const_sems,
    ) = rest_refs[2 * n_consts + 1 :]
    xh_ref, xl_ref, far_h, far_l, fwd_h, fwd_l, back_h, back_l, small = held
    devices = n_py * n_pz
    local = NX // 2 // devices
    rows = devices * ROWS
    per_row = NX // BN
    cells = CY * CZ
    my_y, my_z = lax.axis_index("py"), lax.axis_index("pz")
    me = my_y * n_pz + my_z
    slots = w_ref.shape[0]
    chunks = slots // CHUNK
    barrier = pltpu.get_barrier_semaphore()

    def fetch(k):
        here = pl.ds(k * CHUNK, CHUNK)
        return pltpu.make_async_copy(w_ref.at[here], near_ref.at[here], sems.at[k])

    for k in range(chunks):
        fetch(k).start()
    loads = [
        pltpu.make_async_copy(c, h, const_sems.at[i]) for i, (c, h) in enumerate(zip(consts, held))
    ]
    for load in loads:
        load.start()
    vel_ref[...] = jnp.zeros_like(vel_ref)
    recv_a[...] = jnp.zeros_like(recv_a)
    recv_b[...] = jnp.zeros_like(recv_b)

    def greet(k, carry):
        other = lax.rem(me + k, devices)
        pl.semaphore_signal(
            barrier, inc=1, device_id=(other // n_pz, lax.rem(other, n_pz)), device_id_type=MESH
        )
        return carry

    lax.fori_loop(1, devices, greet, 0)

    sent = pl.ds(0, local)

    def exchange(send, recv, phase):
        order = list(range(1, devices))
        turns = [lax.rem(my_y + k, n_py) for k in range(n_py)]
        if n_py == 4:
            order = list(range(devices - n_pz)) + list(range(devices - n_pz + 1, devices))
            turns = [3 - my_y, turns[2], 3 - turns[2], my_y]
        for k in order:
            to_y = turns[k // n_pz]
            to_z = lax.rem(my_z + k % n_pz, n_pz)
            pltpu.make_async_remote_copy(
                src_ref=send.at[to_y * n_pz + to_z, sent],
                dst_ref=recv.at[me, sent],
                send_sem=send_sem.at[phase],
                recv_sem=recv_sem.at[phase],
                device_id=(to_y, to_z),
                device_id_type=MESH,
            ).start()

    def finish(send, recv, phase):
        many = pl.ds(0, devices - 1)
        pltpu.make_async_copy(recv.at[many, sent], recv.at[many, sent], recv_sem.at[phase]).wait()

    def drain(send, phase):
        many = pl.ds(0, devices - 1)
        pltpu.make_async_copy(send.at[many, sent], send.at[many, sent], send_sem.at[phase]).wait()

    picks[...] = jnp.zeros_like(picks)
    parts[...] = jnp.zeros_like(parts)
    for b in range(PB_DEV):
        parts[b * ROWS : b * ROWS + 3, :] = parts_ref[:, b * BP : (b + 1) * BP].astype(f32)
    row = lax.broadcasted_iota(jnp.int32, (PB_DEV, slots), 0)
    chooser = jnp.where(row == part_ref[...], 1.0, 0.0).T.astype(bf16)
    for c in range(3):
        block = parts[pl.ds(c, PB_DEV, stride=ROWS), :].astype(bf16)
        picks[pl.ds(c, slots, stride=ROWS), :] = dot(chooser, block)
    near_half = left_half((ROWS, 128))

    def chunk(k, carry):
        fetch(k).wait()
        for g in range(CHUNK // GROUP):
            first = k * CHUNK + g * GROUP
            picked = picks[pl.ds(first * ROWS, GROUP * ROWS), :]
            tiles = near_ref[pl.ds(first, GROUP)].reshape(GROUP * BN, BP)
            got = dot(picked.astype(bf16), tiles, ((1,), (1,)))
            own = []
            for i in range(GROUP):
                lanes = i // 2 * 128
                keep = near_half if i % 2 == 0 else ~near_half
                piece = got[i * ROWS : (i + 1) * ROWS, lanes : lanes + 128]
                own.append(jnp.where(keep, piece, 0.0))
            pairs[pl.ds(first * ROWS, GROUP * ROWS), :] = jnp.concatenate(own, axis=0)
        return carry

    lax.fori_loop(0, chunks, chunk, 0)
    for load in loads:
        load.wait()
    row = lax.broadcasted_iota(jnp.int32, (cells * per_row, slots), 0)
    block = row % cells * per_row + row // cells
    live = lax.broadcasted_iota(jnp.int32, (cells * per_row, slots), 1) < count[0]
    hits = jnp.where((block == node_ref[...]) & live, 1.0, 0.0).astype(bf16)
    left = left_half((cells, 128))
    lines = []
    for c in range(3):
        high, rest = split(pairs[pl.ds(c, slots, stride=ROWS), :])
        total = dot(hits, high) + dot(hits, rest)
        total += pltpu.roll(total, BN, 1)
        pieces = [
            jnp.where(
                left, total[xb * cells : (xb + 1) * cells], total[(xb + 1) * cells : (xb + 2) * cells]
            )
            for xb in range(0, per_row, 2)
        ]
        lines.append(jnp.concatenate(pieces, axis=1))
    vort = jnp.concatenate(lines, axis=0)
    low = jnp.concatenate([vort, jnp.zeros((80, NX), f32)], axis=0)
    up = jnp.concatenate([jnp.zeros((64, NX), f32), vort, jnp.zeros((16, NX), f32)], axis=0)
    over = ((1,), (1,))
    modes = jnp.zeros((rows, 128), f32)
    for k, field in ((0, low), (1, up)):
        high, rest = split(field)
        modes += dot(xh_ref[k], high, over) + (
            dot(xh_ref[k], rest, over) + dot(xl_ref[k], high, over)
        )
    send_a[...] = modes.reshape(devices, ROWS, 128)
    recv_a[me] = send_a[me]
    pl.semaphore_wait(barrier, devices - 1)
    exchange(send_a, recv_a, 0)

    def spread_out(i):
        return jnp.broadcast_to(small[i][:, None, :], (devices, ROWS, 128)).reshape(rows, 128)

    slot = lax.broadcasted_iota(jnp.int32, (rows, 128), 0) % ROWS
    mode = me * local + slot
    wave_x = mode.astype(f32) * (2.0 * math.pi / NX)
    total = spread_out(2) + wave_x * wave_x
    ny_nz = CY * n_py * CZ * n_pz
    weight = jnp.where(mode == 0, 1.0, 2.0) * (1.0 / (NX * ny_nz))
    inverse = spread_out(7) * weight / jnp.where(total > 0, total, 1.0)
    gain_a = (spread_out(3) + wave_x * spread_out(5)) * inverse
    gain_b = (spread_out(4) + wave_x * spread_out(6)) * inverse
    turn_cos, turn_sin = spread_out(0), spread_out(1)
    sign = jnp.where(lax.broadcasted_iota(jnp.int32, (rows, 128), 1) < 64, 1.0, -1.0)

    def swap(x):
        return pltpu.roll(x, 64, 1)

    def across(x):
        high, rest = split(x)
        both = dot(far_h[...], high) + (dot(far_h[...], rest) + dot(far_l[...], high))
        return both[:rows], swap(both[rows:]) * sign

    def along(x, table_h, table_l):
        high, rest = split(x)
        return dot(high, table_h[...]) + (dot(rest, table_h[...]) + dot(high, table_l[...]))

    finish(send_a, recv_a, 0)
    even, odd = across(recv_a[...].reshape(rows, 128))
    y = even + odd
    z = turn_cos * y + turn_sin * swap(y)
    both = along(z, fwd_h, fwd_l)
    vel = gain_a * both[:, :128] - gain_b * both[:, 128:]
    y = along(vel, back_h, back_l)
    z = turn_cos * y - turn_sin * swap(y)
    even, odd = across(z)
    send_b[...] = (even - odd).reshape(devices, ROWS, 128)
    recv_b[me] = send_b[me]
    exchange(send_b, recv_b, 1)
    drain(send_a, 0)
    finish(send_b, recv_b, 1)
    back = recv_b[...].reshape(rows, 128).T
    grid = jnp.zeros((48, NX), f32)
    for k in range(2):
        high, rest = split(back[64 * k : 64 * k + 48])
        grid += dot(high, xh_ref[k]) + (dot(rest, xh_ref[k]) + dot(high, xl_ref[k]))
    grid = grid.astype(bf16).astype(f32)
    for c in range(3):
        for xb in range(0, per_row, 2):
            piece = grid[c * cells : (c + 1) * cells, xb * BN : (xb + 2) * BN]
            other = pltpu.roll(piece, BN, 1)
            for h, both in ((0, jnp.where(left, piece, other)), (1, jnp.where(left, other, piece))):
                where = pl.ds((xb + h) * ROWS + c, cells, stride=per_row * ROWS)
                vel_ref[where, :] = both

    row = lax.broadcasted_iota(jnp.int32, (cells * per_row, slots), 0)
    chooser = jnp.where(row == node_ref[...], 1.0, 0.0).T.astype(bf16)
    for c in range(3):
        block = vel_ref[pl.ds(c, cells * per_row, stride=ROWS), :].astype(bf16)
        picks[pl.ds(c, slots, stride=ROWS), :] = dot(chooser, block)

    def gather(k, carry):
        for g in range(CHUNK // GROUP):
            first = k * CHUNK + g * GROUP
            lines = []
            for i in range(GROUP):
                keep = near_half if i % 2 == 0 else ~near_half
                own = jnp.where(keep, picks[pl.ds((first + i) * ROWS, ROWS), :], 0.0)
                zero = jnp.zeros((ROWS, 128), f32)
                lines.append(
                    jnp.concatenate(
                        [own if h == i // 2 else zero for h in range(GROUP // 2)], axis=1
                    )
                )
            chosen = jnp.concatenate(lines, axis=0).astype(bf16)
            tiles = near_ref[pl.ds(first, GROUP)].reshape(GROUP * BN, BP)
            pairs[pl.ds(first * ROWS, GROUP * ROWS), :] = dot(chosen, tiles)
        return carry

    lax.fori_loop(0, chunks, gather, 0)
    row = lax.broadcasted_iota(jnp.int32, (PB_DEV, slots), 0)
    live = lax.broadcasted_iota(jnp.int32, (PB_DEV, slots), 1) < count[0]
    hits = jnp.where((row == part_ref[...]) & live, 1.0, 0.0).astype(bf16)
    for c in range(3):
        high, rest = split(pairs[pl.ds(c, slots, stride=ROWS), :])
        out_ref[c] = dot(hits, high) + dot(hits, rest)
    drain(send_b, 1)


def solve_direct(vort_p, weights, part, node, counts, n_py, n_pz):
    devices = n_py * n_pz
    node_blocks = NX * CY * CZ // BN
    slots = weights.shape[0]
    smem = pl.BlockSpec(memory_space=pltpu.SMEM)
    vmem = pl.BlockSpec(memory_space=pltpu.VMEM)
    hbm = pl.BlockSpec(memory_space=pltpu.HBM)
    block = pltpu.VMEM((devices, ROWS, 128), f32)
    consts = tables(n_py, n_pz)
    consts = [jnp.asarray(t) for t in consts]
    out = pl.pallas_call(
        functools.partial(solve_kernel, n_py, n_pz),
        out_shape=jax.ShapeDtypeStruct((3, PB_DEV, BP), f32),
        in_specs=[smem, vmem, vmem, vmem, hbm] + [hbm] * len(consts),
        out_specs=vmem,
        scratch_shapes=[
            *[pltpu.VMEM(t.shape, t.dtype) for t in consts],
            pltpu.VMEM(weights.shape, weights.dtype),
            pltpu.VMEM((node_blocks * ROWS, 2 * BN), f32),
            block,
            block,
            block,
            block,
            pltpu.SemaphoreType.DMA((2,)),
            pltpu.SemaphoreType.DMA((2,)),
            pltpu.VMEM((PB_DEV * ROWS, BP), f32),
            pltpu.VMEM((slots * ROWS, 128), f32),
            pltpu.VMEM((slots * ROWS, 128), f32),
            pltpu.SemaphoreType.DMA((slots // CHUNK,)),
            pltpu.SemaphoreType.DMA((len(consts),)),
        ],
        compiler_params=pltpu.CompilerParams(
            collective_id=0, has_side_effects=True, vmem_limit_bytes=60 * 2**20
        ),
        name="solve",
    )(counts, part[None], node[None], vort_p, weights, *consts)
    return out.reshape(3, PB_DEV * BP)


def solve_staged(sums, n_py, n_pz):
    highest = lax.Precision.HIGHEST
    node_blocks = sums.shape[0]
    y_cells, z_cells = CY * n_py, CZ * n_pz
    x_modes = NX // 2
    sums = sums[:, :3, :BN] + sums[:, :3, BN:]
    vort_grid = sums.transpose(1, 0, 2).reshape(3, CZ, CY, NX)
    angle_fwd = twiddle(jnp.arange(NX), jnp.arange(x_modes), NX)
    x_forward = jnp.stack([jnp.cos(angle_fwd), -jnp.sin(angle_fwd)], 1)
    angle_inv = twiddle(jnp.arange(x_modes), jnp.arange(NX), NX)
    mode_weight = (jnp.where(jnp.arange(x_modes) == 0, 1.0, 2.0) / NX)[:, None]
    x_inverse = jnp.stack([mode_weight * jnp.cos(angle_inv), -mode_weight * jnp.sin(angle_inv)], 0)
    y_forward = forward_table(y_cells)
    z_forward = forward_table(z_cells)
    z_inverse = inverse_table(z_cells)
    y_inverse = inverse_table(y_cells)
    x_spectrum = jnp.einsum("czyx,xrm->czrmy", vort_grid, x_forward, precision=highest)
    row_section = jnp.einsum(
        "czrmy,rysk->cmskz",
        lax.all_to_all(x_spectrum, "py", split_axis=3, concat_axis=4, tiled=True),
        y_forward,
        precision=highest,
    )
    col_section = jnp.einsum(
        "cmrkz,rzsw->cmskw",
        lax.all_to_all(row_section, "pz", split_axis=3, concat_axis=4, tiled=True),
        z_forward,
        precision=highest,
    )
    vel_spectrum = curl_solve(col_section, y_cells, z_cells)
    z_back = jnp.einsum("cmrkw,rwsz->cmszk", vel_spectrum, z_inverse, precision=highest)
    y_back = jnp.einsum(
        "cmrzk,rksy->czsym",
        lax.all_to_all(z_back, "pz", split_axis=3, concat_axis=4, tiled=True),
        y_inverse,
        precision=highest,
    )
    vel_grid = jnp.einsum(
        "czrym,rmx->czyx",
        lax.all_to_all(y_back, "py", split_axis=3, concat_axis=4, tiled=True),
        x_inverse,
        precision=highest,
    )
    vel_nodes = vel_grid.astype(bf16).astype(f32).reshape(3, node_blocks, BN).transpose(1, 0, 2)
    vel_nodes = jnp.concatenate([vel_nodes, vel_nodes], axis=2)
    return jnp.pad(vel_nodes, ((0, 0), (0, ROWS - 3), (0, 0)))


def per_device(vort_p, pair_weights, pair_part, pair_node, counts):
    n_py, n_pz = lax.axis_size("py"), lax.axis_size("pz")
    node_blocks = NX * CY * CZ // BN
    devices, x_modes = n_py * n_pz, NX // 2
    if devices <= 32 and x_modes % devices == 0 and x_modes // devices <= ROWS:
        return solve_direct(vort_p, pair_weights, pair_part, pair_node, counts, n_py, n_pz)
    sums, near = spread(vort_p, pair_weights, pair_part, pair_node, counts, node_blocks)
    vel = solve_staged(sums, n_py, n_pz)
    return collect(vel, near, pair_part, pair_node, counts)


def solution(mesh):
    placed = (
        P(None, ("py", "pz")),
        P(("py", "pz"), None, None),
        P(("py", "pz")),
        P(("py", "pz")),
        P(("py", "pz")),
    )
    return jax.shard_map(
        per_device, mesh=mesh, in_specs=placed, out_specs=P(None, ("py", "pz")), check_vma=False
    )
```

profile of v0, /device:TPU:0, one launch (start us, length us, event | category | flops | bytes accessed | tf_op | source)
XLA Modules:
  0.0 25.2 jit_solution(16608775270704185995)
XLA Ops:
  0.7 23.1 %solve.1 = f32[3,32,128]{2,1,0:T(8,128)} custom-call(s32[1]{0:T(128)S(6)} %copy.18.count, s32[1,256]{1,0:T(1,128)} %bitcast.7, s32[1,256]{1,0:T(1,128)} %bitcast.8, bf16[3,4096]{1,0:T(4,128)(2,1)} %parts_ref.1, bf16[256,64,128]{2,1,0:T(8,128)(2,1)} %w_ref.1, bf16[2,256,384]{2,1,0:T(8,128)(2,1)} %constant.18.clone.rest_refs_0_, ...), custom_call_target="tpu_custom_call" | custom-call | tf_op jit(solution)/shard_map/solve/pallas_call | solution.py:507
  23.8 1.5 %copy.17 = f32[1,3,32,128]{3,1,2,0:T(4,128)} copy(f32[1,3,32,128]{3,2,1,0:T(8,128)} %bitcast.6) | data formatting | bytes 98304
where the time goes:
time: 25.5 us; the launch traced here: 25.2 us
  Pallas kernels  23.1 us (91%)
  local copies, waits for them, and re-layouts  1.46 us (6%)
  between operations  0.66 us (3%)
    pallas_call x1, Pallas kernels, solve_direct(): pl.pallas_call(functools.partial(solve_kernel, n_py, n_pz), out_shape=jax...  23.1 us
    unnamed x1, local copies, waits for them, and re-layouts  1.46 us

commit v1 on v0

v1 whole, which is shorter than its diff:
```python
import functools
import math

import jax
import jax.numpy as jnp
import numpy as np
from jax import lax
from jax.experimental import pallas as pl
from jax.experimental.pallas import tpu as pltpu
from jax.sharding import PartitionSpec as P

NX = 384
CY = 8
CZ = 2
BP = 128
BN = 64
PB_DEV = 32
ROWS = 8
CHUNK = 32
GROUP = 4
N_PY = 4
N_PZ = 8
MESH = pl.DeviceIdType.MESH
f32 = jnp.float32
bf16 = jnp.bfloat16


def twiddle(row_index, col_index, period):
    product = row_index[:, None] * col_index[None, :] % period
    return product.astype(jnp.float32) * (2.0 * math.pi / period)


def forward_table(length):
    angle = twiddle(jnp.arange(length), jnp.arange(length), length)
    cosine = jnp.cos(angle)
    sines = jnp.sin(angle)
    return jnp.stack([jnp.stack([cosine, -sines], 1), jnp.stack([sines, cosine], 1)], 0)


def inverse_table(length):
    angle = twiddle(jnp.arange(length), jnp.arange(length), length)
    cosine = jnp.cos(angle) / length
    sines = jnp.sin(angle) / length
    return jnp.stack([jnp.stack([cosine, sines], 1), jnp.stack([-sines, cosine], 1)], 0)


def cross_terms(coeffs, field):
    return jnp.stack(
        [
            coeffs[1] * field[2] - coeffs[2] * field[1],
            coeffs[2] * field[0] - coeffs[0] * field[2],
            coeffs[0] * field[1] - coeffs[1] * field[0],
        ],
        axis=0,
    )


def signed_wave(length, index):
    signed = jnp.where(index < length // 2, index, index - length)
    return (signed.astype(jnp.float32) * (2.0 * math.pi / length), index == length // 2)


def curl_solve(spectrum, y_cells, z_cells):
    x_local = spectrum.shape[1]
    y_local = spectrum.shape[3]
    mode_x = lax.axis_index("py") * x_local + jnp.arange(x_local)
    wave_x = mode_x.astype(jnp.float32) * (2.0 * math.pi / NX)
    wave_y, edge_y = signed_wave(y_cells, lax.axis_index("pz") * y_local + jnp.arange(y_local))
    wave_z, edge_z = signed_wave(z_cells, jnp.arange(z_cells))
    wave_x3 = wave_x[:, None, None]
    wave_y3 = wave_y[None, :, None]
    wave_z3 = wave_z[None, None, :]
    total = wave_x3 * wave_x3 + wave_y3 * wave_y3 + wave_z3 * wave_z3
    edges = edge_y[None, :, None] | edge_z[None, None, :]
    keep = (total > 0) & jnp.logical_not(edges)
    inverse_sq = jnp.where(keep, 1.0 / jnp.where(keep, total, 1.0), 0.0)
    inv_wave = (wave_x3 * inverse_sq, wave_y3 * inverse_sq, wave_z3 * inverse_sq)
    real_turn = cross_terms(inv_wave, spectrum[:, :, 0])
    imag_turn = cross_terms(inv_wave, spectrum[:, :, 1])
    return jnp.stack([-imag_turn, real_turn], axis=2)


def halves(table):
    table = np.asarray(table, np.float32)
    high = table.astype(bf16)
    return high, (table - high.astype(np.float32)).astype(bf16)


def split(x):
    high = x.astype(bf16)
    return high, (x - high.astype(f32)).astype(bf16)


def dot(a, b, dims=((1,), (0,))):
    return lax.dot_general(a, b, (dims, ((), ())), preferred_element_type=f32)


def left_half(shape):
    return lax.broadcasted_iota(jnp.int32, shape, 1) < BN


def spread_kernel(part, node, count, parts_ref, w_ref, out_ref, near_ref, parts, sems):
    chunks = w_ref.shape[0] // CHUNK

    def fetch(k):
        here = pl.ds(k * CHUNK, CHUNK)
        return pltpu.make_async_copy(w_ref.at[here], near_ref.at[here], sems.at[k])

    for k in range(chunks):
        fetch(k).start()
    out_ref[...] = jnp.zeros_like(out_ref)
    parts[...] = jnp.zeros_like(parts)
    for b in range(PB_DEV):
        parts[b, 0:3, :] = parts_ref[:, b * BP : (b + 1) * BP].astype(f32)
    left = left_half((ROWS, 128))

    def chunk(k, carry):
        fetch(k).wait()
        base = k * CHUNK
        for g in range(CHUNK // GROUP):
            first = base + g * GROUP
            picked = jnp.concatenate([parts[part[first + i]] for i in range(GROUP)], axis=0)
            tiles = near_ref[pl.ds(first, GROUP)].reshape(GROUP * BN, BP)
            got = dot(picked.astype(bf16), tiles, ((1,), (1,)))
            for i in range(GROUP):
                keep = jnp.logical_and(left if i % 2 == 0 else ~left, first + i < count[0])
                lanes = i // 2 * 128
                own = got[i * ROWS : (i + 1) * ROWS, lanes : lanes + 128]
                out_ref[node[first + i]] += jnp.where(keep, own, 0.0)
        return carry

    lax.fori_loop(0, chunks, chunk, 0)


def spread(vort_p, weights, part, node, counts, node_blocks):
    smem = pl.BlockSpec(memory_space=pltpu.SMEM)
    vmem = pl.BlockSpec(memory_space=pltpu.VMEM)
    return pl.pallas_call(
        spread_kernel,
        out_shape=(
            jax.ShapeDtypeStruct((node_blocks, ROWS, 2 * BN), f32),
            jax.ShapeDtypeStruct(weights.shape, weights.dtype),
        ),
        in_specs=[smem, smem, smem, vmem, pl.BlockSpec(memory_space=pltpu.HBM)],
        out_specs=(vmem, vmem),
        scratch_shapes=[
            pltpu.VMEM((PB_DEV, ROWS, BP), f32),
            pltpu.SemaphoreType.DMA((weights.shape[0] // CHUNK,)),
        ],
        compiler_params=pltpu.CompilerParams(vmem_limit_bytes=48 * 2**20),
        name="spread",
    )(part, node, counts, vort_p, weights)


def collect_kernel(part, node, count, vel_ref, w_ref, out_ref, sums):
    sums[...] = jnp.zeros_like(sums)
    left = left_half((ROWS, 128))
    zero = jnp.zeros((ROWS, 128), f32)

    def chunk(k, carry):
        for g in range(CHUNK // GROUP):
            first = k * CHUNK + g * GROUP
            rows = []
            for i in range(GROUP):
                slot = first + i
                keep = jnp.logical_and(left if i % 2 == 0 else ~left, slot < count[0])
                own = jnp.where(keep, vel_ref[node[slot]], 0.0)
                rows.append(
                    jnp.concatenate(
                        [own if h == i // 2 else zero for h in range(GROUP // 2)], axis=1
                    )
                )
            chosen = jnp.concatenate(rows, axis=0).astype(bf16)
            got = dot(chosen, w_ref[pl.ds(first, GROUP)].reshape(GROUP * BN, BP))
            for i in range(GROUP):
                sums[part[first + i]] += got[i * ROWS : (i + 1) * ROWS]
        return carry

    lax.fori_loop(0, w_ref.shape[0] // CHUNK, chunk, 0)
    for b in range(PB_DEV):
        out_ref[:, b * BP : (b + 1) * BP] = sums[b, 0:3, :]


def collect(vel, weights, part, node, counts):
    smem = pl.BlockSpec(memory_space=pltpu.SMEM)
    vmem = pl.BlockSpec(memory_space=pltpu.VMEM)
    return pl.pallas_call(
        collect_kernel,
        out_shape=jax.ShapeDtypeStruct((3, PB_DEV * BP), f32),
        in_specs=[smem, smem, smem, vmem, vmem],
        out_specs=vmem,
        scratch_shapes=[pltpu.VMEM((PB_DEV, ROWS, BP), f32)],
        compiler_params=pltpu.CompilerParams(vmem_limit_bytes=24 * 2**20),
        name="collect",
    )(part, node, counts, vel, weights)


def tables():
    devices = N_PY * N_PZ
    local = NX // 2 // devices
    ny, nz = CY * N_PY, CZ * N_PZ
    row = np.arange(devices * ROWS)
    slot, device = row % ROWS, row // ROWS
    mode = device * local + slot
    angle = 2 * np.pi * (mode[:, None] * np.arange(NX)[None] % NX) / NX
    used = (slot < local)[:, None]
    x_cos, x_sin = np.where(used, np.cos(angle), 0.0), np.where(used, -np.sin(angle), 0.0)
    index = np.arange(devices)
    a, b = index // N_PZ, index % N_PZ
    lane = np.arange(128)
    real, comp, cell = lane // 64, lane % 64 // 16, lane % 16
    zl, yl = cell // CY, cell % CY
    valid = (comp < 3)[None]
    phi = 2 * np.pi * (a[:, None] * yl[None] / ny + b[:, None] * zl[None] / nz)
    sign = np.where(real == 0, 1.0, -1.0)[None]
    turn_cos, turn_sin = np.cos(phi), np.sin(phi) * sign
    psi = 2 * np.pi * (yl[:, None] * yl[None] / CY + zl[:, None] * zl[None] / CZ)
    cosine, sines = np.cos(psi), np.sin(psi)
    r, q = real[:, None], real[None]

    def near(ahead):
        both = np.where(r == q, sines, np.where(r == 0, cosine, -cosine))
        same = (comp[:, None] == (comp[None] + ahead) % 3) & (comp[:, None] < 3) & valid
        return np.where(same, both, 0.0)

    forward = np.concatenate([near(2), near(1)], 1)
    both = np.where(r == q, cosine, np.where(r == 0, sines, -sines))
    same = (comp[:, None] == comp[None]) & (comp[:, None] < 3)
    back = np.where(same, both, 0.0)
    my, mz = a[:, None] + N_PY * yl[None], b[:, None] + N_PZ * zl[None]
    keep = (my != ny // 2) & (mz != nz // 2) & valid
    my, mz = np.where(my < ny // 2, my, my - ny), np.where(mz < nz // 2, mz, mz - nz)
    ky, kz = 2 * np.pi * my / ny, 2 * np.pi * mz / nz
    zero = np.zeros_like(ky)
    wave = np.stack([zero, ky, kz])
    k_first = np.where(comp == 0, wave[1], np.where(comp == 1, wave[2], wave[0]))
    k_second = np.where(comp == 0, wave[2], np.where(comp == 1, wave[0], wave[1]))
    x_first = np.broadcast_to(comp == 2, ky.shape)
    x_second = np.broadcast_to(comp == 1, ky.shape)
    small = [turn_cos, turn_sin, ky * ky + kz * kz, k_first, k_second, x_first, x_second, keep]
    small = np.stack(small).astype(np.float32)
    near_table = np.concatenate([forward, back], 1)
    near_high = near_table.astype(np.float32).astype(bf16)
    return [
        *halves(np.concatenate([x_cos, x_sin], 1)),
        np.concatenate([near_high, near_high], 0),
        small,
    ]


def flip(index, bits):
    for bit in (1, 2, 4):
        if bits & bit:
            index = index + bit - 2 * bit * (index // bit % 2)
    return index


def swap(x):
    return pltpu.roll(x, 64, 1)


def line_transform(x, turn):
    if len(x) == 2:
        return [x[0] + x[1], x[0] - x[1]]
    half = len(x) // 2
    even = [x[k] + x[k + half] for k in range(half)]
    odd = [x[k] - x[k + half] for k in range(half)]
    if half == 2:
        side = turn(odd[1])
        low, high = line_transform(even, turn), [odd[0] + side, odd[0] - side]
    else:
        side = turn(odd[2])
        near, far = odd[1] - odd[3], turn(odd[1] + odd[3])
        root = math.sqrt(0.5)
        plus, minus = (near + far) * root, (far - near) * root
        first, second = odd[0] + side, odd[0] - side
        low = line_transform(even, turn)
        high = [first + plus, second + minus, first - plus, second - minus]
    return [value for pair in zip(low, high) for value in pair]


def plane_transform(blocks, turn):
    columns = [
        line_transform([blocks[a * N_PZ + b] for a in range(N_PY)], turn) for b in range(N_PZ)
    ]
    lines = [line_transform([columns[b][a] for b in range(N_PZ)], turn) for a in range(N_PY)]
    return [lines[a][b] for a in range(N_PY) for b in range(N_PZ)]


def solve_kernel(
    count,
    part_hbm,
    node_hbm,
    parts_hbm,
    w_ref,
    xh_hbm,
    xl_hbm,
    near_hbm,
    small_hbm,
    near_ref,
    vel_ref,
    choose_ref,
    gather_ref,
    part_ref,
    node_ref,
    parts_ref,
    xh_ref,
    xl_ref,
    tab_ref,
    small,
    send_a,
    recv_a,
    send_b,
    recv_b,
    send_sem,
    recv_sem,
    parts,
    picks,
    pairs,
    held,
    sems,
    const_sems,
    first_sems,
):
    devices = N_PY * N_PZ
    local = NX // 2 // devices
    rows = devices * ROWS
    per_row = NX // BN
    cells = CY * CZ
    groups = w_ref.shape[1]
    slots = GROUP * groups
    chunks = sems.shape[0]
    step = groups // chunks
    my_y, my_z = lax.axis_index("py"), lax.axis_index("pz")
    me = my_y * N_PZ + my_z
    others = [
        (flip(my_y, ky), flip(my_z, kz))
        for ky in (2, 3, 1, 0)
        for kz in range(N_PZ - 1, -1, -1)
        if ky or kz
    ]

    def fetch(k):
        here = pl.ds(k * step, step)
        return pltpu.make_async_copy(w_ref.at[:, here], near_ref.at[:, here], sems.at[k])

    firsts = [
        pltpu.make_async_copy(c, h, first_sems.at[i])
        for i, (c, h) in enumerate(
            ((parts_hbm, parts_ref), (part_hbm, part_ref), (node_hbm, node_ref))
        )
    ]
    for load in firsts:
        load.start()
    for k in range(chunks):
        fetch(k).start()
    if not False:
        barrier = pltpu.get_barrier_semaphore()
        for other in others:
            pl.semaphore_signal(barrier, inc=1, device_id=other, device_id_type=MESH)
    loads = [
        pltpu.make_async_copy(c, h, const_sems.at[i])
        for i, (c, h) in enumerate(
            ((xh_hbm, xh_ref), (xl_hbm, xl_ref), (near_hbm, tab_ref), (small_hbm, small))
        )
    ]
    for load in loads:
        load.start()

    sent = pl.ds(0, local)

    def exchange(send, recv, phase):
        if False:
            recv[...] = send[...]
            return
        for to_y, to_z in others:
            pltpu.make_async_remote_copy(
                src_ref=send.at[to_y * N_PZ + to_z, sent],
                dst_ref=recv.at[me, sent],
                send_sem=send_sem.at[phase],
                recv_sem=recv_sem.at[phase],
                device_id=(to_y, to_z),
                device_id_type=MESH,
            ).start()

    def wait_all(buffer, sem):
        if False:
            return
        many = pl.ds(0, devices - 1)
        pltpu.make_async_copy(buffer.at[many, sent], buffer.at[many, sent], sem).wait()

    def stop(value):
        vel_ref[...] = jnp.zeros_like(vel_ref) + value.astype(bf16)
        choose_ref[...] = jnp.zeros_like(choose_ref)
        gather_ref[...] = jnp.zeros_like(gather_ref)

    def wait_fetches():
        for k in range(chunks):
            fetch(k).wait()
        for load in loads:
            load.wait()

    for load in firsts:
        load.wait()
    if 0 == 1:
        wait_fetches()
        return stop(jnp.zeros((1, 128), f32))

    for b in range(PB_DEV):
        parts[b * ROWS : b * ROWS + 3, :] = parts_ref[:, b * BP : (b + 1) * BP].astype(f32)
    row = lax.broadcasted_iota(jnp.int32, (PB_DEV, slots), 0)
    chooser = jnp.where(row == part_ref[...], 1.0, 0.0).T.astype(bf16)
    tall = GROUP * 4
    for c in range(3):
        block = parts[pl.ds(c, PB_DEV, stride=ROWS), :].astype(bf16)
        got = dot(chooser, block)
        for i in range(GROUP):
            here = pl.ds(c * GROUP + i, groups, stride=tall)
            picks[here, :] = got[i * groups : (i + 1) * groups]
    if 0 == 2:
        wait_fetches()
        return stop(picks[0:1])
    if 0 == 3:
        wait_fetches()
    sub = lax.broadcasted_iota(jnp.int32, (tall, 128), 0) % GROUP
    half = lax.broadcasted_iota(jnp.int32, (tall, 128), 1) // BN
    low_slots = sub < 2
    own_half = sub % 2 == half
    for k in range(chunks):
        if 0 != 3:
            fetch(k).wait()
        for g in range(k * step, (k + 1) * step):
            picked = picks[g * tall : (g + 1) * tall, :].astype(bf16)
            tiles = near_ref[:, g].reshape(GROUP * BN, BP)
            got = dot(picked, tiles, ((1,), (1,)))
            own = jnp.where(low_slots, got[:, :128], got[:, 128:])
            pairs[g * tall : (g + 1) * tall, :] = jnp.where(own_half, own, 0.0)
    if 0 != 3:
        for load in loads:
            load.wait()
    if 0 == 3 or 0 == 4:
        return stop(pairs[0:1])

    def pairs_of(c):
        return jnp.concatenate(
            [pairs[pl.ds(c * GROUP + i, groups, stride=tall), :] for i in range(GROUP)], axis=0
        )

    row = lax.broadcasted_iota(jnp.int32, (cells * per_row, slots), 0)
    block = row % cells * per_row + row // cells
    live = lax.broadcasted_iota(jnp.int32, (cells * per_row, slots), 1) < count[0]
    hits = jnp.where((block == node_ref[...]) & live, 1.0, 0.0)
    choose_ref[...] = hits.T.astype(bf16)
    hits = hits.astype(bf16)
    left = left_half((cells, 128))
    lines = []
    for c in range(3):
        total = dot(hits, jnp.concatenate(split(pairs_of(c)), axis=1))
        total = total[:, :128] + total[:, 128:]
        total += swap(total)
        pieces = [
            jnp.where(
                left, total[xb * cells : (xb + 1) * cells], total[(xb + 1) * cells : (xb + 2) * cells]
            )
            for xb in range(0, per_row, 2)
        ]
        lines.append(jnp.concatenate(pieces, axis=1))
    vort = jnp.concatenate([*lines, jnp.zeros((cells, NX), f32)], axis=0)
    if 0 == 5:
        return stop(vort[0:1, 0:128])
    high, rest = split(vort)
    none = jnp.zeros_like(high)
    both = [
        jnp.concatenate(
            [jnp.concatenate([x, none], axis=1), jnp.concatenate([none, x], axis=1)], axis=0
        )
        for x in (high, rest)
    ]
    over = ((1,), (1,))
    modes = dot(xh_ref[...], jnp.concatenate(both, axis=0), over)
    modes = modes[:, :128] + (modes[:, 128:] + dot(xl_ref[...], both[0], over))
    send_a[...] = modes.reshape(devices, ROWS, 128)
    recv_a[me] = send_a[me]
    if 0 == 6:
        return stop(send_a[0, 0:1])
    if not False:
        pl.semaphore_wait(barrier, devices - 1)
    exchange(send_a, recv_a, 0)

    unsent = jnp.zeros((devices, ROWS - local, 128), f32)
    recv_b[:, local:, :] = unsent
    row = lax.broadcasted_iota(jnp.int32, (PB_DEV, slots), 0)
    live = lax.broadcasted_iota(jnp.int32, (PB_DEV, slots), 1) < count[0]
    gather_ref[...] = jnp.where((row == part_ref[...]) & live, 1.0, 0.0).astype(bf16)

    def spread_out(i):
        return jnp.broadcast_to(small[i][:, None, :], (devices, ROWS, 128)).reshape(rows, 128)

    slot = lax.broadcasted_iota(jnp.int32, (rows, 128), 0) % ROWS
    mode = me * local + slot
    wave_x = mode.astype(f32) * (2.0 * math.pi / NX)
    total = spread_out(2) + wave_x * wave_x
    weight = jnp.where(mode == 0, 1.0, 2.0) * (1.0 / (NX * CY * N_PY * CZ * N_PZ))
    inverse = spread_out(7) * weight / jnp.where(total > 0, total, 1.0)
    held[0] = (spread_out(3) + wave_x * spread_out(5)) * inverse
    held[1] = (spread_out(4) + wave_x * spread_out(6)) * inverse
    held[2], held[3] = spread_out(0), spread_out(1)
    sign = jnp.where(lax.broadcasted_iota(jnp.int32, (ROWS, 128), 1) < 64, 1.0, -1.0)

    def ahead(x):
        return swap(x) * sign

    def astern(x):
        return swap(x) * -sign

    def along(x, table):
        return dot(jnp.concatenate(split(x), axis=1), table)

    wait_all(recv_a, recv_sem.at[0])
    if 0 == 7:
        return stop(recv_a[0, 0:1] + held[0, 0:1] + held[1, 0:1] + held[2, 0:1] + held[3, 0:1])
    y = plane_transform([recv_a[d] for d in range(devices)], ahead)
    y = jnp.concatenate(y, axis=0)
    if 0 == 8:
        send_b[...] = y.reshape(devices, ROWS, 128)
        return stop(send_b[0, 0:1])
    z = held[2] * y + held[3] * swap(y)
    both = along(z, tab_ref[:, 0:256])
    if 0 == 9:
        send_b[...] = (both[:, :128] + both[:, 128:]).reshape(devices, ROWS, 128)
        return stop(send_b[0, 0:1])
    vel = held[0] * both[:, :128] - held[1] * both[:, 128:]
    y = along(vel, tab_ref[:, 256:384])
    z = held[2] * y - held[3] * swap(y)
    if 0 == 10:
        send_b[...] = z.reshape(devices, ROWS, 128)
        return stop(send_b[0, 0:1])
    z = plane_transform([z[d * ROWS : (d + 1) * ROWS] for d in range(devices)], astern)
    for d in range(devices):
        send_b[d] = z[d]
    recv_b[me, 0:local] = send_b[me, 0:local]
    if 0 == 11:
        return stop(send_b[0, 0:1])
    exchange(send_b, recv_b, 1)
    wait_all(send_a, send_sem.at[0])
    wait_all(recv_b, recv_sem.at[1])
    back = recv_b[...].reshape(rows, 128).T
    grid = jnp.zeros((48, NX), f32)
    for k in range(2):
        high, rest = split(back[64 * k : 64 * k + 48])
        table = xh_ref[:, k * NX : (k + 1) * NX]
        both = dot(jnp.concatenate([high, rest], axis=0), table)
        grid += both[:48] + (both[48:] + dot(high, xl_ref[:, k * NX : (k + 1) * NX]))
    if 0 == 12:
        return stop(grid[0:1, 0:128])
    for c in range(3):
        for xb in range(0, per_row, 2):
            piece = grid[c * cells : (c + 1) * cells, xb * BN : (xb + 2) * BN]
            other = swap(piece)
            for h, line in ((0, jnp.where(left, piece, other)), (1, jnp.where(left, other, piece))):
                vel_ref[c, (xb + h) * cells : (xb + h + 1) * cells, :] = line.astype(bf16)
    wait_all(send_b, send_sem.at[1])


def collect_kernel_b(vel_ref, choose_ref, gather_ref, w_ref, out_ref, picks, pairs, sums):
    groups = w_ref.shape[1]
    tall = GROUP * 4
    picks[...] = jnp.zeros_like(picks)
    chooser = choose_ref[...]
    for c in range(3):
        got = dot(chooser, vel_ref[c])
        for i in range(GROUP):
            here = pl.ds(c * GROUP + i, groups, stride=tall)
            picks[here, :] = got[i * groups : (i + 1) * groups]
    sub = lax.broadcasted_iota(jnp.int32, (tall, 128), 0) % GROUP
    half = lax.broadcasted_iota(jnp.int32, (tall, 128), 1) // BN
    first = (sub < 2) & (sub % 2 == half)
    second = (sub >= 2) & (sub % 2 == half)
    for g in range(groups):
        line = picks[g * tall : (g + 1) * tall, :]
        chosen = jnp.concatenate([jnp.where(first, line, 0.0), jnp.where(second, line, 0.0)], axis=1)
        pairs[g * tall : (g + 1) * tall, :] = dot(
            chosen.astype(bf16), w_ref[:, g].reshape(GROUP * BN, BP)
        )
    for c in range(3):
        lines = jnp.concatenate(
            [pairs[pl.ds(c * GROUP + i, groups, stride=tall), :] for i in range(GROUP)], axis=0
        )
        total = dot(gather_ref[...], jnp.concatenate(split(lines), axis=1))
        sums[pl.ds(c, PB_DEV, stride=ROWS), :] = total[:, :128] + total[:, 128:]
    for b in range(PB_DEV):
        out_ref[:, b * BP : (b + 1) * BP] = sums[b * ROWS : b * ROWS + 3, :]


def solve_direct(vort_p, weights, part, node, counts):
    devices = N_PY * N_PZ
    node_blocks = NX * CY * CZ // BN
    slots = weights.shape[0]
    groups = slots // GROUP
    vmem = pl.BlockSpec(memory_space=pltpu.VMEM)
    hbm = pl.BlockSpec(memory_space=pltpu.HBM)
    block = pltpu.VMEM((devices, ROWS, 128), f32)
    consts = [jnp.asarray(t) for t in tables()]
    weights = weights.reshape(GROUP, groups, BN, BP)
    inputs = [part[None], node[None], vort_p, weights, *consts]
    tall = pltpu.VMEM((groups * GROUP * 4, 128), f32)
    near, vel, chooser, gather = pl.pallas_call(
        solve_kernel,
        out_shape=(
            jax.ShapeDtypeStruct(weights.shape, weights.dtype),
            jax.ShapeDtypeStruct((3, node_blocks, 128), bf16),
            jax.ShapeDtypeStruct((slots, node_blocks), bf16),
            jax.ShapeDtypeStruct((PB_DEV, slots), bf16),
        ),
        in_specs=[pl.BlockSpec(memory_space=pltpu.SMEM)] + [hbm] * len(inputs),
        out_specs=(vmem, vmem, vmem, vmem),
        scratch_shapes=[
            pltpu.VMEM((1, slots), jnp.int32),
            pltpu.VMEM((1, slots), jnp.int32),
            pltpu.VMEM(vort_p.shape, vort_p.dtype),
            *[pltpu.VMEM(t.shape, t.dtype) for t in consts],
            block,
            block,
            block,
            block,
            pltpu.SemaphoreType.DMA((2,)),
            pltpu.SemaphoreType.DMA((2,)),
            pltpu.VMEM((PB_DEV * ROWS, BP), f32),
            tall,
            tall,
            pltpu.VMEM((4, devices * ROWS, 128), f32),
            pltpu.SemaphoreType.DMA((8,)),
            pltpu.SemaphoreType.DMA((len(consts),)),
            pltpu.SemaphoreType.DMA((3,)),
        ],
        compiler_params=pltpu.CompilerParams(
            collective_id=None if False else 0, has_side_effects=True, vmem_limit_bytes=24 * 2**20
        ),
        name="solve",
    )(counts, *[pltpu.with_memory_space_constraint(x, pltpu.HBM) for x in inputs])
    return pl.pallas_call(
        collect_kernel_b,
        out_shape=jax.ShapeDtypeStruct((3, PB_DEV * BP), f32),
        in_specs=[vmem] * 4,
        out_specs=vmem,
        scratch_shapes=[tall, tall, pltpu.VMEM((PB_DEV * ROWS, BP), f32)],
        compiler_params=pltpu.CompilerParams(vmem_limit_bytes=16 * 2**20),
        name="collect_last",
    )(vel, chooser, gather, near)


def solve_staged(sums, n_py, n_pz):
    highest = lax.Precision.HIGHEST
    node_blocks = sums.shape[0]
    y_cells, z_cells = CY * n_py, CZ * n_pz
    x_modes = NX // 2
    sums = sums[:, :3, :BN] + sums[:, :3, BN:]
    vort_grid = sums.transpose(1, 0, 2).reshape(3, CZ, CY, NX)
    angle_fwd = twiddle(jnp.arange(NX), jnp.arange(x_modes), NX)
    x_forward = jnp.stack([jnp.cos(angle_fwd), -jnp.sin(angle_fwd)], 1)
    angle_inv = twiddle(jnp.arange(x_modes), jnp.arange(NX), NX)
    mode_weight = (jnp.where(jnp.arange(x_modes) == 0, 1.0, 2.0) / NX)[:, None]
    x_inverse = jnp.stack([mode_weight * jnp.cos(angle_inv), -mode_weight * jnp.sin(angle_inv)], 0)
    y_forward = forward_table(y_cells)
    z_forward = forward_table(z_cells)
    z_inverse = inverse_table(z_cells)
    y_inverse = inverse_table(y_cells)
    x_spectrum = jnp.einsum("czyx,xrm->czrmy", vort_grid, x_forward, precision=highest)
    row_section = jnp.einsum(
        "czrmy,rysk->cmskz",
        lax.all_to_all(x_spectrum, "py", split_axis=3, concat_axis=4, tiled=True),
        y_forward,
        precision=highest,
    )
    col_section = jnp.einsum(
        "cmrkz,rzsw->cmskw",
        lax.all_to_all(row_section, "pz", split_axis=3, concat_axis=4, tiled=True),
        z_forward,
        precision=highest,
    )
    vel_spectrum = curl_solve(col_section, y_cells, z_cells)
    z_back = jnp.einsum("cmrkw,rwsz->cmszk", vel_spectrum, z_inverse, precision=highest)
    y_back = jnp.einsum(
        "cmrzk,rksy->czsym",
        lax.all_to_all(z_back, "pz", split_axis=3, concat_axis=4, tiled=True),
        y_inverse,
        precision=highest,
    )
    vel_grid = jnp.einsum(
        "czrym,rmx->czyx",
        lax.all_to_all(y_back, "py", split_axis=3, concat_axis=4, tiled=True),
        x_inverse,
        precision=highest,
    )
    vel_nodes = vel_grid.astype(bf16).astype(f32).reshape(3, node_blocks, BN).transpose(1, 0, 2)
    vel_nodes = jnp.concatenate([vel_nodes, vel_nodes], axis=2)
    return jnp.pad(vel_nodes, ((0, 0), (0, ROWS - 3), (0, 0)))


def per_device(vort_p, pair_weights, pair_part, pair_node, counts):
    n_py, n_pz = lax.axis_size("py"), lax.axis_size("pz")
    node_blocks = NX * CY * CZ // BN
    if (n_py, n_pz) == (N_PY, N_PZ):
        return solve_direct(vort_p, pair_weights, pair_part, pair_node, counts)
    sums, near = spread(vort_p, pair_weights, pair_part, pair_node, counts, node_blocks)
    vel = solve_staged(sums, n_py, n_pz)
    return collect(vel, near, pair_part, pair_node, counts)


def solution(mesh):
    placed = (
        P(None, ("py", "pz")),
        P(("py", "pz"), None, None),
        P(("py", "pz")),
        P(("py", "pz")),
        P(("py", "pz")),
    )
    return jax.shard_map(
        per_device, mesh=mesh, in_specs=placed, out_specs=P(None, ("py", "pz")), check_vma=False
    )
```

time: 25.5 us -> 20.9 us (0.82)
  Pallas kernels: 23.1 us -> 20.1 us
  local copies, waits for them, and re-layouts: 1.46 us -> 0 us
    pallas_call x1 -> x2, Pallas kernels: 23.1 us -> 20.1 us  [the longest x1 18.3 us: solve_direct(): pl.pallas_call(solve_kernel, out_shape=(jax.ShapeDtypeStruct(weights.shap...]
    unnamed x1 -> x0, local copies, waits for them, and re-layouts: 1.46 us -> none
where the time goes in v1:
time: 20.9 us; the launch traced here: 20.7 us
  Pallas kernels  20.1 us (96%)
  between operations  0.66 us (3%)
    pallas_call x1, Pallas kernels, solve_direct(): pl.pallas_call(solve_kernel, out_shape=(jax.ShapeDtypeStruct(weights.shap...  18.3 us
    pallas_call x1, Pallas kernels, solve_direct(): pl.pallas_call(collect_kernel_b, out_shape=jax.ShapeDtypeStruct((3, PB_DE...  1.76 us

profile of v1, /device:TPU:0, one launch (start us, length us, event | category | flops | bytes accessed | tf_op | source)
XLA Modules:
  0.0 20.7 jit_solution(15235222656469406809)
XLA Ops:
  0.7 18.3 %solve.1 = (bf16[4,64,64,128]{3,2,1,0:T(8,128)(2,1)S(1)}, bf16[3,96,128]{2,1,0:T(8,128)(2,1)S(1)}, bf16[256,96]{1,0:T(8,128)(2,1)S(1)}, bf16[32,256]{1,0:T(8,128)(2,1)S(1)}) custom-call(s32[1]{0:T(128)S(6)} %copy.10.count, s32[1,256]{1,0:T(1,128)} %bitcast.4, s32[1,256]{1,0:T(1,128)} %bitcast.5, bf16[3,4096]{1,0:T(4,128)(2,1)} %parts_hbm.1, ...), custom_call_target="tpu_custom_call" | custom-call | tf_op jit(solution)/shard_map/solve/pallas_call | solution.py:607
  19.0 1.8 %collect_last.1 = f32[3,4096]{1,0:T(4,128)} custom-call(bf16[3,96,128]{2,1,0:T(8,128)(2,1)S(1)} %get-tuple-element.9.vel_ref, bf16[256,96]{1,0:T(8,128)(2,1)S(1)} %get-tuple-element.10.choose_ref, bf16[32,256]{1,0:T(8,128)(2,1)S(1)} %get-tuple-element.11.gather_ref, bf16[4,64,64,128]{3,2,1,0:T(8,128)(2,1)S(1)} %get-tuple-element.12.w_ref), custom_call_target="tpu_custom_call" | custom-call | tf_op jit(solution)/shard_map/collect_last/pallas_call | solution.py:641

commit v2 on v1

--- a/solution.py
+++ b/solution.py
@@ -193,6 +193,9 @@
         compiler_params=pltpu.CompilerParams(vmem_limit_bytes=24 * 2**20),
         name="collect",
     )(part, node, counts, vel, weights)
+
+
+ORDER = [(2, 6), (3, 6), (3, 7), (2, 7), (2, 3), (1, 7), (1, 6), (2, 2), (3, 2), (3, 4), (3, 5), (3, 3), (2, 5), (2, 4), (1, 5), (1, 4), (0, 7), (1, 3), (2, 1), (0, 6), (1, 2), (3, 1), (3, 0), (2, 0), (1, 0), (0, 3), (1, 1), (0, 4), (0, 5), (0, 2), (0, 1)]
 
 
 def tables():
@@ -333,12 +336,7 @@
     step = groups // chunks
     my_y, my_z = lax.axis_index("py"), lax.axis_index("pz")
     me = my_y * N_PZ + my_z
-    others = [
-        (flip(my_y, ky), flip(my_z, kz))
-        for ky in (2, 3, 1, 0)
-        for kz in range(N_PZ - 1, -1, -1)
-        if ky or kz
-    ]
+    others = [(flip(my_y, ky), flip(my_z, kz)) for ky, kz in ORDER]
 
     def fetch(k):
         here = pl.ds(k * step, step)
@@ -629,7 +627,7 @@
             tall,
             tall,
             pltpu.VMEM((4, devices * ROWS, 128), f32),
-            pltpu.SemaphoreType.DMA((8,)),
+            pltpu.SemaphoreType.DMA((2,)),
             pltpu.SemaphoreType.DMA((len(consts),)),
             pltpu.SemaphoreType.DMA((3,)),
         ],

time: 20.9 us -> 20 us (0.957)
  Pallas kernels: 20.1 us -> 19.2 us
    pallas_call x1, Pallas kernels: 18.3 us -> 17.4 us  [solve_direct(): pl.pallas_call(solve_kernel, out_shape=(jax.ShapeDtypeStruct(weights.shap...]
where the time goes in v2:
time: 20 us; the launch traced here: 19.8 us
  Pallas kernels  19.2 us (96%)
  between operations  0.66 us (3%)
    pallas_call x1, Pallas kernels, solve_direct(): pl.pallas_call(solve_kernel, out_shape=(jax.ShapeDtypeStruct(weights.shap...  17.4 us
    pallas_call x1, Pallas kernels, solve_direct(): pl.pallas_call(collect_kernel_b, out_shape=jax.ShapeDtypeStruct((3, PB_DE...  1.76 us

profile of v2, /device:TPU:0, one launch (start us, length us, event | category | flops | bytes accessed | tf_op | source)
XLA Modules:
  0.0 19.8 jit_solution(239588496072566161)
XLA Ops:
  0.7 17.4 %solve.1 = (bf16[4,64,64,128]{3,2,1,0:T(8,128)(2,1)S(1)}, bf16[3,96,128]{2,1,0:T(8,128)(2,1)S(1)}, bf16[256,96]{1,0:T(8,128)(2,1)S(1)}, bf16[32,256]{1,0:T(8,128)(2,1)S(1)}) custom-call(s32[1]{0:T(128)S(6)} %copy.10.count, s32[1,256]{1,0:T(1,128)} %bitcast.4, s32[1,256]{1,0:T(1,128)} %bitcast.5, bf16[3,4096]{1,0:T(4,128)(2,1)} %parts_hbm.1, ...), custom_call_target="tpu_custom_call" | custom-call | tf_op jit(solution)/shard_map/solve/pallas_call | solution.py:605
  18.1 1.8 %collect_last.1 = f32[3,4096]{1,0:T(4,128)} custom-call(bf16[3,96,128]{2,1,0:T(8,128)(2,1)S(1)} %get-tuple-element.9.vel_ref, bf16[256,96]{1,0:T(8,128)(2,1)S(1)} %get-tuple-element.10.choose_ref, bf16[32,256]{1,0:T(8,128)(2,1)S(1)} %get-tuple-element.11.gather_ref, bf16[4,64,64,128]{3,2,1,0:T(8,128)(2,1)S(1)} %get-tuple-element.12.w_ref), custom_call_target="tpu_custom_call" | custom-call | tf_op jit(solution)/shard_map/collect_last/pallas_call | solution.py:639

commit v3 on v2

--- a/solution.py
+++ b/solution.py
@@ -195,15 +195,24 @@
     )(part, node, counts, vel, weights)
 
 
-ORDER = [(2, 6), (3, 6), (3, 7), (2, 7), (2, 3), (1, 7), (1, 6), (2, 2), (3, 2), (3, 4), (3, 5), (3, 3), (2, 5), (2, 4), (1, 5), (1, 4), (0, 7), (1, 3), (2, 1), (0, 6), (1, 2), (3, 1), (3, 0), (2, 0), (1, 0), (0, 3), (1, 1), (0, 4), (0, 5), (0, 2), (0, 1)]
+EDGES = (0, 28, 64)
+MIDS = 2 * N_PZ
+TALL = 16
+PARTNERS = (6, 7, 4, 5, 2, 3, 1, 0)
+HOPS = {0: 0, 1: 0, 2: 1, 3: 1, 4: 1, 5: 1, 6: 2, 7: 2}
+
+
+def by_hops(planes):
+    pairs = [(plane, kz) for plane in range(len(planes)) for kz in PARTNERS]
+    return sorted(pairs, key=lambda pair: -(planes[pair[0]] + HOPS[pair[1]]))
 
 
 def tables():
     devices = N_PY * N_PZ
-    local = NX // 2 // devices
+    local = NX // 2 // MIDS
     ny, nz = CY * N_PY, CZ * N_PZ
-    row = np.arange(devices * ROWS)
-    slot, device = row % ROWS, row // ROWS
+    row = np.arange(MIDS * TALL)
+    slot, device = row % TALL, row // TALL
     mode = device * local + slot
     angle = 2 * np.pi * (mode[:, None] * np.arange(NX)[None] % NX) / NX
     used = (slot < local)[:, None]
@@ -245,7 +254,7 @@
     near_table = np.concatenate([forward, back], 1)
     near_high = near_table.astype(np.float32).astype(bf16)
     return [
-        *halves(np.concatenate([x_cos, x_sin], 1)),
+        np.concatenate(halves(np.concatenate([x_cos, x_sin], 1)), 1),
         np.concatenate([near_high, near_high], 0),
         small,
     ]
@@ -282,22 +291,13 @@
     return [value for pair in zip(low, high) for value in pair]
 
 
-def plane_transform(blocks, turn):
-    columns = [
-        line_transform([blocks[a * N_PZ + b] for a in range(N_PY)], turn) for b in range(N_PZ)
-    ]
-    lines = [line_transform([columns[b][a] for b in range(N_PZ)], turn) for a in range(N_PY)]
-    return [lines[a][b] for a in range(N_PY) for b in range(N_PZ)]
-
-
 def solve_kernel(
     count,
     part_hbm,
     node_hbm,
     parts_hbm,
     w_ref,
-    xh_hbm,
-    xl_hbm,
+    x_hbm,
     near_hbm,
     small_hbm,
     near_ref,
@@ -307,8 +307,7 @@
     part_ref,
     node_ref,
     parts_ref,
-    xh_ref,
-    xl_ref,
+    x_ref,
     tab_ref,
     small,
     send_a,
@@ -324,22 +323,30 @@
     sems,
     const_sems,
     first_sems,
+    plane_sem,
 ):
     devices = N_PY * N_PZ
-    local = NX // 2 // devices
-    rows = devices * ROWS
+    local = NX // 2 // MIDS
+    rows = devices * TALL
     per_row = NX // BN
     cells = CY * CZ
     groups = w_ref.shape[1]
     slots = GROUP * groups
     chunks = sems.shape[0]
-    step = groups // chunks
     my_y, my_z = lax.axis_index("py"), lax.axis_index("pz")
     me = my_y * N_PZ + my_z
-    others = [(flip(my_y, ky), flip(my_z, kz)) for ky, kz in ORDER]
+    mid = (my_y == 1) | (my_y == 2)
+    outer = jnp.logical_not(mid)
+    my_mid = me - N_PZ
+    near_plane, far_plane = 1 + my_y // 2, 2 - my_y // 2
+    opposite = 6 - 3 * my_y
+    mid_planes = (opposite, 3 - opposite, 3 - my_y, my_y)
+    to_mids = [((far_plane, near_plane)[p], flip(my_z, kz)) for p, kz in by_hops((2, 1))]
+    order = [pair for pair in by_hops((2, 1, 1, 0)) if pair != (3, 0)]
+    to_all = [(mid_planes[p], flip(my_z, kz)) for p, kz in order]
 
     def fetch(k):
-        here = pl.ds(k * step, step)
+        here = pl.ds(EDGES[k], EDGES[k + 1] - EDGES[k])
         return pltpu.make_async_copy(w_ref.at[:, here], near_ref.at[:, here], sems.at[k])
 
     firsts = [
@@ -354,38 +361,60 @@
         fetch(k).start()
     if not False:
         barrier = pltpu.get_barrier_semaphore()
-        for other in others:
-            pl.semaphore_signal(barrier, inc=1, device_id=other, device_id_type=MESH)
+
+        @pl.when(mid)
+        def _():
+            for other in to_all:
+                pl.semaphore_signal(barrier, inc=1, device_id=other, device_id_type=MESH)
+
+        @pl.when(outer)
+        def _():
+            for other in to_mids:
+                pl.semaphore_signal(barrier, inc=1, device_id=other, device_id_type=MESH)
+
     loads = [
         pltpu.make_async_copy(c, h, const_sems.at[i])
         for i, (c, h) in enumerate(
-            ((xh_hbm, xh_ref), (xl_hbm, xl_ref), (near_hbm, tab_ref), (small_hbm, small))
+            ((x_hbm, x_ref), (near_hbm, tab_ref), (small_hbm, small))
         )
     ]
-    for load in loads:
-        load.start()
-
-    sent = pl.ds(0, local)
-
-    def exchange(send, recv, phase):
-        if False:
-            recv[...] = send[...]
-            return
-        for to_y, to_z in others:
-            pltpu.make_async_remote_copy(
-                src_ref=send.at[to_y * N_PZ + to_z, sent],
-                dst_ref=recv.at[me, sent],
-                send_sem=send_sem.at[phase],
-                recv_sem=recv_sem.at[phase],
-                device_id=(to_y, to_z),
-                device_id_type=MESH,
-            ).start()
-
-    def wait_all(buffer, sem):
-        if False:
-            return
-        many = pl.ds(0, devices - 1)
-        pltpu.make_async_copy(buffer.at[many, sent], buffer.at[many, sent], sem).wait()
+
+    packed = 3 * local // 4
+    sent = pl.ds(0, packed)
+    spare = lax.broadcasted_iota(jnp.int32, (1, 128), 1) % 64 // 16
+
+    def pack(buffer, first, many):
+        lines = buffer.reshape(buffer.shape[0] * TALL, 128)
+        for j in range(local - packed):
+            extra = lines[pl.ds(first * TALL + packed + j, many, stride=TALL), :]
+            for c in range(3):
+                here = pl.ds(first * TALL + 3 * j + c, many, stride=TALL)
+                moved = pltpu.roll(extra, 16 * (3 - c), 1)
+                lines[here, :] = jnp.where(spare == 3, moved, lines[here, :])
+
+    def unpack(buffer, first, many):
+        lines = buffer.reshape(buffer.shape[0] * TALL, 128)
+        for j in range(local - packed):
+            extra = jnp.zeros((many, 128), f32)
+            for c in range(3):
+                line = lines[pl.ds(first * TALL + 3 * j + c, many, stride=TALL), :]
+                moved = pltpu.roll(line, 128 - 16 * (3 - c), 1)
+                extra = jnp.where(spare == c, moved, extra)
+            lines[pl.ds(first * TALL + packed + j, many, stride=TALL), :] = extra
+
+    def push(source, target, phase, landed, device):
+        pltpu.make_async_remote_copy(
+            src_ref=source.at[sent],
+            dst_ref=target.at[sent],
+            send_sem=send_sem.at[phase],
+            recv_sem=landed,
+            device_id=device,
+            device_id_type=MESH,
+        ).start()
+
+    def wait_blocks(buffer, many, sem):
+        blocks = buffer.at[pl.ds(0, many), sent]
+        pltpu.make_async_copy(blocks, blocks, sem).wait()
 
     def stop(value):
         vel_ref[...] = jnp.zeros_like(vel_ref) + value.astype(bf16)
@@ -401,6 +430,8 @@
     for load in firsts:
         load.wait()
     if 0 == 1:
+        for load in loads:
+            load.start()
         wait_fetches()
         return stop(jnp.zeros((1, 128), f32))
 
@@ -425,18 +456,19 @@
     low_slots = sub < 2
     own_half = sub % 2 == half
     for k in range(chunks):
-        if 0 != 3:
-            fetch(k).wait()
-        for g in range(k * step, (k + 1) * step):
+        fetch(k).wait()
+        if k == 0:
+            for load in loads:
+                load.start()
+        for g in range(EDGES[k], EDGES[k + 1]):
             picked = picks[g * tall : (g + 1) * tall, :].astype(bf16)
             tiles = near_ref[:, g].reshape(GROUP * BN, BP)
             got = dot(picked, tiles, ((1,), (1,)))
             own = jnp.where(low_slots, got[:, :128], got[:, 128:])
             pairs[g * tall : (g + 1) * tall, :] = jnp.where(own_half, own, 0.0)
-    if 0 != 3:
+    if 0 == 3 or 0 == 4:
         for load in loads:
             load.wait()
-    if 0 == 3 or 0 == 4:
         return stop(pairs[0:1])
 
     def pairs_of(c):
@@ -464,7 +496,10 @@
         ]
         lines.append(jnp.concatenate(pieces, axis=1))
     vort = jnp.concatenate([*lines, jnp.zeros((cells, NX), f32)], axis=0)
+    loads[0].wait()
     if 0 == 5:
+        for load in loads[1:]:
+            load.wait()
         return stop(vort[0:1, 0:128])
     high, rest = split(vort)
     none = jnp.zeros_like(high)
@@ -475,35 +510,47 @@
         for x in (high, rest)
     ]
     over = ((1,), (1,))
-    modes = dot(xh_ref[...], jnp.concatenate(both, axis=0), over)
-    modes = modes[:, :128] + (modes[:, 128:] + dot(xl_ref[...], both[0], over))
-    send_a[...] = modes.reshape(devices, ROWS, 128)
-    recv_a[me] = send_a[me]
+    modes = dot(x_ref[:, : 2 * NX], jnp.concatenate(both, axis=0), over)
+    modes = modes[:, :128] + (modes[:, 128:] + dot(x_ref[:, 2 * NX :], both[0], over))
+    send_a[...] = modes.reshape(MIDS, TALL, 128)
+    pack(send_a, 0, MIDS)
     if 0 == 6:
+        for load in loads[1:]:
+            load.wait()
         return stop(send_a[0, 0:1])
+
+    def push_modes(device):
+        to_y, to_z = device
+        push(send_a.at[(to_y - 1) * N_PZ + to_z], recv_a.at[me], 0, plane_sem.at[my_y], device)
+
     if not False:
-        pl.semaphore_wait(barrier, devices - 1)
-    exchange(send_a, recv_a, 0)
-
-    unsent = jnp.zeros((devices, ROWS - local, 128), f32)
-    recv_b[:, local:, :] = unsent
+
+        @pl.when(mid)
+        def _():
+            pl.semaphore_wait(barrier, devices - 1)
+
+        @pl.when(outer)
+        def _():
+            pl.semaphore_wait(barrier, MIDS)
+
+        for device in to_mids[:-1]:
+            push_modes(device)
+
+        @pl.when(outer)
+        def _():
+            push_modes(to_mids[-1])
+
+    for load in loads[1:]:
+        load.wait()
+    recv_b[:, local:, :] = jnp.zeros((MIDS, TALL - local, 128), f32)
     row = lax.broadcasted_iota(jnp.int32, (PB_DEV, slots), 0)
     live = lax.broadcasted_iota(jnp.int32, (PB_DEV, slots), 1) < count[0]
     gather_ref[...] = jnp.where((row == part_ref[...]) & live, 1.0, 0.0).astype(bf16)
 
     def spread_out(i):
-        return jnp.broadcast_to(small[i][:, None, :], (devices, ROWS, 128)).reshape(rows, 128)
-
-    slot = lax.broadcasted_iota(jnp.int32, (rows, 128), 0) % ROWS
-    mode = me * local + slot
-    wave_x = mode.astype(f32) * (2.0 * math.pi / NX)
-    total = spread_out(2) + wave_x * wave_x
-    weight = jnp.where(mode == 0, 1.0, 2.0) * (1.0 / (NX * CY * N_PY * CZ * N_PZ))
-    inverse = spread_out(7) * weight / jnp.where(total > 0, total, 1.0)
-    held[0] = (spread_out(3) + wave_x * spread_out(5)) * inverse
-    held[1] = (spread_out(4) + wave_x * spread_out(6)) * inverse
-    held[2], held[3] = spread_out(0), spread_out(1)
-    sign = jnp.where(lax.broadcasted_iota(jnp.int32, (ROWS, 128), 1) < 64, 1.0, -1.0)
+        return jnp.broadcast_to(small[i][:, None, :], (devices, TALL, 128)).reshape(rows, 128)
+
+    sign = jnp.where(lax.broadcasted_iota(jnp.int32, (TALL, 128), 1) < 64, 1.0, -1.0)
 
     def ahead(x):
         return swap(x) * sign
@@ -514,41 +561,93 @@
     def along(x, table):
         return dot(jnp.concatenate(split(x), axis=1), table)
 
-    wait_all(recv_a, recv_sem.at[0])
-    if 0 == 7:
-        return stop(recv_a[0, 0:1] + held[0, 0:1] + held[1, 0:1] + held[2, 0:1] + held[3, 0:1])
-    y = plane_transform([recv_a[d] for d in range(devices)], ahead)
-    y = jnp.concatenate(y, axis=0)
-    if 0 == 8:
-        send_b[...] = y.reshape(devices, ROWS, 128)
-        return stop(send_b[0, 0:1])
-    z = held[2] * y + held[3] * swap(y)
-    both = along(z, tab_ref[:, 0:256])
-    if 0 == 9:
-        send_b[...] = (both[:, :128] + both[:, 128:]).reshape(devices, ROWS, 128)
-        return stop(send_b[0, 0:1])
-    vel = held[0] * both[:, :128] - held[1] * both[:, 128:]
-    y = along(vel, tab_ref[:, 256:384])
-    z = held[2] * y - held[3] * swap(y)
-    if 0 == 10:
-        send_b[...] = z.reshape(devices, ROWS, 128)
-        return stop(send_b[0, 0:1])
-    z = plane_transform([z[d * ROWS : (d + 1) * ROWS] for d in range(devices)], astern)
-    for d in range(devices):
-        send_b[d] = z[d]
-    recv_b[me, 0:local] = send_b[me, 0:local]
-    if 0 == 11:
-        return stop(send_b[0, 0:1])
-    exchange(send_b, recv_b, 1)
-    wait_all(send_a, send_sem.at[0])
-    wait_all(recv_b, recv_sem.at[1])
-    back = recv_b[...].reshape(rows, 128).T
+    def solve_modes():
+        slot = lax.broadcasted_iota(jnp.int32, (rows, 128), 0) % TALL
+        mode = my_mid * local + slot
+        wave_x = mode.astype(f32) * (2.0 * math.pi / NX)
+        total = spread_out(2) + wave_x * wave_x
+        weight = jnp.where(mode == 0, 1.0, 2.0) * (1.0 / (NX * CY * N_PY * CZ * N_PZ))
+        inverse = spread_out(7) * weight / jnp.where(total > 0, total, 1.0)
+        held[0] = (spread_out(3) + wave_x * spread_out(5)) * inverse
+        held[1] = (spread_out(4) + wave_x * spread_out(6)) * inverse
+        held[2], held[3] = spread_out(0), spread_out(1)
+        if False:
+            recv_a[0:MIDS] = send_a[...]
+            recv_a[MIDS:] = send_a[...]
+        else:
+            recv_a[me] = send_a[my_mid]
+            recv_a[:, local:, :] = jnp.zeros((devices, TALL - local, 128), f32)
+        planes = (
+            (my_y, N_PZ - 1), (3 - my_y, N_PZ), (3 - opposite, N_PZ), (opposite, N_PZ)
+        )
+        for plane, many in planes:
+            if not False:
+                wait_blocks(recv_a, many, plane_sem.at[plane])
+            first = plane * N_PZ
+            unpack(recv_a, first, N_PZ)
+            line = line_transform([recv_a[first + b] for b in range(N_PZ)], ahead)
+            for b in range(N_PZ):
+                recv_a[first + b] = line[b]
+        if 0 == 7:
+            return
+        columns = [
+            line_transform([recv_a[a * N_PZ + b] for a in range(N_PY)], ahead) for b in range(N_PZ)
+        ]
+        y = jnp.concatenate([columns[b][a] for a in range(N_PY) for b in range(N_PZ)], axis=0)
+        z = held[2] * y + held[3] * swap(y)
+        both = along(z, tab_ref[:, 0:256])
+        vel = held[0] * both[:, :128] - held[1] * both[:, 128:]
+        y = along(vel, tab_ref[:, 256:384])
+        z = held[2] * y - held[3] * swap(y)
+        z = [z[d * TALL : (d + 1) * TALL] for d in range(devices)]
+        columns = [
+            line_transform([z[a * N_PZ + b] for a in range(N_PY)], astern) for b in range(N_PZ)
+        ]
+        for plane in (0, 3, 1, 2):
+            line = line_transform([columns[b][plane] for b in range(N_PZ)], astern)
+            for b in range(N_PZ):
+                send_b[plane * N_PZ + b] = line[b]
+            pack(send_b, plane * N_PZ, N_PZ)
+            if not False:
+                for kz in PARTNERS[:-1]:
+                    push_cells(plane, flip(my_z, kz))
+                if plane in (0, 3):
+                    push_cells(plane, my_z)
+                else:
+                    pl.when(my_y != plane)(functools.partial(push_cells, plane, my_z))
+        recv_b[my_mid, 0:packed] = send_b[me, 0:packed]
+
+    def push_cells(to_y, to_z):
+        source = send_b.at[to_y * N_PZ + to_z]
+        push(source, recv_b.at[my_mid], 1, recv_sem.at[1], (to_y, to_z))
+
+    if False:
+        solve_modes()
+        if 0 == 7:
+            return stop(recv_a[0, 0:1] + held[0, 0:1] + held[1, 0:1] + held[2, 0:1] + held[3, 0:1])
+        if 0 == 11:
+            return stop(send_b[0, 0:1])
+    else:
+
+        @pl.when(mid)
+        def _():
+            solve_modes()
+            wait_blocks(send_a, MIDS - 1, send_sem.at[0])
+            wait_blocks(recv_b, MIDS - 1, recv_sem.at[1])
+
+        @pl.when(outer)
+        def _():
+            wait_blocks(send_a, MIDS, send_sem.at[0])
+            wait_blocks(recv_b, MIDS, recv_sem.at[1])
+
+    unpack(recv_b, 0, MIDS)
+    back = recv_b[...].reshape(MIDS * TALL, 128).T
     grid = jnp.zeros((48, NX), f32)
     for k in range(2):
         high, rest = split(back[64 * k : 64 * k + 48])
-        table = xh_ref[:, k * NX : (k + 1) * NX]
+        table = x_ref[:, k * NX : (k + 1) * NX]
         both = dot(jnp.concatenate([high, rest], axis=0), table)
-        grid += both[:48] + (both[48:] + dot(high, xl_ref[:, k * NX : (k + 1) * NX]))
+        grid += both[:48] + (both[48:] + dot(high, x_ref[:, (k + 2) * NX : (k + 3) * NX]))
     if 0 == 12:
         return stop(grid[0:1, 0:128])
     for c in range(3):
@@ -557,7 +656,11 @@
             other = swap(piece)
             for h, line in ((0, jnp.where(left, piece, other)), (1, jnp.where(left, other, piece))):
                 vel_ref[c, (xb + h) * cells : (xb + h + 1) * cells, :] = line.astype(bf16)
-    wait_all(send_b, send_sem.at[1])
+    if not False:
+
+        @pl.when(mid)
+        def _():
+            wait_blocks(send_b, devices - 1, send_sem.at[1])
 
 
 def collect_kernel_b(vel_ref, choose_ref, gather_ref, w_ref, out_ref, picks, pairs, sums):
@@ -597,7 +700,7 @@
     groups = slots // GROUP
     vmem = pl.BlockSpec(memory_space=pltpu.VMEM)
     hbm = pl.BlockSpec(memory_space=pltpu.HBM)
-    block = pltpu.VMEM((devices, ROWS, 128), f32)
+    all_blocks, mid_blocks = (pltpu.VMEM((n, TALL, 128), f32) for n in (devices, MIDS))
     consts = [jnp.asarray(t) for t in tables()]
     weights = weights.reshape(GROUP, groups, BN, BP)
     inputs = [part[None], node[None], vort_p, weights, *consts]
@@ -617,19 +720,20 @@
             pltpu.VMEM((1, slots), jnp.int32),
             pltpu.VMEM(vort_p.shape, vort_p.dtype),
             *[pltpu.VMEM(t.shape, t.dtype) for t in consts],
-            block,
-            block,
-            block,
-            block,
+            mid_blocks,
+            all_blocks,
+            all_blocks,
+            mid_blocks,
             pltpu.SemaphoreType.DMA((2,)),
             pltpu.SemaphoreType.DMA((2,)),
             pltpu.VMEM((PB_DEV * ROWS, BP), f32),
             tall,
             tall,
-            pltpu.VMEM((4, devices * ROWS, 128), f32),
+            pltpu.VMEM((4, devices * TALL, 128), f32),
             pltpu.SemaphoreType.DMA((2,)),
             pltpu.SemaphoreType.DMA((len(consts),)),
             pltpu.SemaphoreType.DMA((3,)),
+            pltpu.SemaphoreType.DMA((N_PY,)),
         ],
         compiler_params=pltpu.CompilerParams(
             collective_id=None if False else 0, has_side_effects=True, vmem_limit_bytes=24 * 2**20

time: 20 us -> 19.7 us (0.985)
  Pallas kernels: 19.2 us -> 18.8 us
    pallas_call x1, Pallas kernels: 17.4 us -> 17.1 us  [solve_direct(): pl.pallas_call(solve_kernel, out_shape=(jax.ShapeDtypeStruct(weights.shap...]
where the time goes in v3:
time: 19.7 us; the launch traced here: 19.5 us
  Pallas kernels  18.8 us (95%)
  between operations  0.66 us (3%)
    pallas_call x1, Pallas kernels, solve_direct(): pl.pallas_call(solve_kernel, out_shape=(jax.ShapeDtypeStruct(weights.shap...  17.1 us
    pallas_call x1, Pallas kernels, solve_direct(): pl.pallas_call(collect_kernel_b, out_shape=jax.ShapeDtypeStruct((3, PB_DE...  1.76 us

profile of v3, /device:TPU:0, one launch (start us, length us, event | category | flops | bytes accessed | tf_op | source)
XLA Modules:
  0.0 19.5 jit_solution(16543944050767205659)
XLA Ops:
  0.7 17.1 %solve.1 = (bf16[4,64,64,128]{3,2,1,0:T(8,128)(2,1)S(1)}, bf16[3,96,128]{2,1,0:T(8,128)(2,1)S(1)}, bf16[256,96]{1,0:T(8,128)(2,1)S(1)}, bf16[32,256]{1,0:T(8,128)(2,1)S(1)}) custom-call(s32[1]{0:T(128)S(6)} %copy.9.count, s32[1,256]{1,0:T(1,128)} %bitcast.4, s32[1,256]{1,0:T(1,128)} %bitcast.5, bf16[3,4096]{1,0:T(4,128)(2,1)} %parts_hbm.1, ...), custom_call_target="tpu_custom_call" | custom-call | tf_op jit(solution)/shard_map/solve/pallas_call | solution.py:708
  17.7 1.8 %collect_last.1 = f32[3,4096]{1,0:T(4,128)} custom-call(bf16[3,96,128]{2,1,0:T(8,128)(2,1)S(1)} %get-tuple-element.9.vel_ref, bf16[256,96]{1,0:T(8,128)(2,1)S(1)} %get-tuple-element.10.choose_ref, bf16[32,256]{1,0:T(8,128)(2,1)S(1)} %get-tuple-element.11.gather_ref, bf16[4,64,64,128]{3,2,1,0:T(8,128)(2,1)S(1)} %get-tuple-element.12.w_ref), custom_call_target="tpu_custom_call" | custom-call | tf_op jit(solution)/shard_map/collect_last/pallas_call | solution.py:743

commit v4 on v3

--- a/solution.py
+++ b/solution.py
@@ -609,6 +609,10 @@
                 send_b[plane * N_PZ + b] = line[b]
             pack(send_b, plane * N_PZ, N_PZ)
             if not False:
+                if plane == 0:
+                    for to_z in range(N_PZ):
+                        push_cells(plane, to_z)
+                    continue
                 for kz in PARTNERS[:-1]:
                     push_cells(plane, flip(my_z, kz))
                 if plane in (0, 3):

time: 19.7 us -> 19.5 us (0.990)
  no operation moved by 1% of the time
where the time goes in v4:
time: 19.5 us; the launch traced here: 19.4 us
  Pallas kernels  18.7 us (96%)
  between operations  0.66 us (3%)
    pallas_call x1, Pallas kernels, solve_direct(): pl.pallas_call(solve_kernel, out_shape=(jax.ShapeDtypeStruct(weights.shap...  17 us
    pallas_call x1, Pallas kernels, solve_direct(): pl.pallas_call(collect_kernel_b, out_shape=jax.ShapeDtypeStruct((3, PB_DE...  1.76 us

profile of v4, /device:TPU:0, one launch (start us, length us, event | category | flops | bytes accessed | tf_op | source)
XLA Modules:
  0.0 19.4 jit_solution(13435383563669920056)
XLA Ops:
  0.7 17.0 %solve.1 = (bf16[4,64,64,128]{3,2,1,0:T(8,128)(2,1)S(1)}, bf16[3,96,128]{2,1,0:T(8,128)(2,1)S(1)}, bf16[256,96]{1,0:T(8,128)(2,1)S(1)}, bf16[32,256]{1,0:T(8,128)(2,1)S(1)}) custom-call(s32[1]{0:T(128)S(6)} %copy.9.count, s32[1,256]{1,0:T(1,128)} %bitcast.4, s32[1,256]{1,0:T(1,128)} %bitcast.5, bf16[3,4096]{1,0:T(4,128)(2,1)} %parts_hbm.1, ...), custom_call_target="tpu_custom_call" | custom-call | tf_op jit(solution)/shard_map/solve/pallas_call | solution.py:712
  17.6 1.8 %collect_last.1 = f32[3,4096]{1,0:T(4,128)} custom-call(bf16[3,96,128]{2,1,0:T(8,128)(2,1)S(1)} %get-tuple-element.9.vel_ref, bf16[256,96]{1,0:T(8,128)(2,1)S(1)} %get-tuple-element.10.choose_ref, bf16[32,256]{1,0:T(8,128)(2,1)S(1)} %get-tuple-element.11.gather_ref, bf16[4,64,64,128]{3,2,1,0:T(8,128)(2,1)S(1)} %get-tuple-element.12.w_ref), custom_call_target="tpu_custom_call" | custom-call | tf_op jit(solution)/shard_map/collect_last/pallas_call | solution.py:747
